TPU v7x, 128 devices: a whole 4x4x4 slice. The times are simulated.
128 devices in a mesh: chain: 128 (over z, y, x, core).
Axes of the slice: x: 4, y: 4, z: 4, core: 2. Of those that a mesh axis runs over, the one named last changes fastest.
Arguments:
- sketch: float32 [256, 64, 256], P('chain'), may hold values from -42 to 42
- inv_diag: float32 [256, 256, 256], P('chain'), may hold values from -0.1 to 1.5
- upper: float32 [256, 256, 256], P('chain'), may hold values from -1.5 to 1.5
- lower: float32 [256, 256, 256], P('chain'), may hold values from -1.1 to 1.1
Outputs:
- basis: float32 [256, 64, 256], P('chain')
- r_factor: float32 [64, 64], replicated
All inputs are finite; a program needn't handle non-finite values.
Results may differ from a plain program's by a relative error of at most 0.0003.
Values sent between devices are 32-bit elements; how exact they have to be, the bound alone decides.
A program may use at most 192 MiB of HBM per device.

v0:
```python
import jax
import jax.numpy as jnp
from jax import lax
from jax.sharding import PartitionSpec as P

HIGH = lax.Precision.HIGHEST


def carried_in(part, axis, combine, identity, reverse):
    count = lax.axis_size(axis)
    place = lax.axis_index(axis)
    ahead = count - 1 - place if reverse else place
    gathered = jax.tree.map(lambda a: lax.all_gather(a, axis), part)
    state = jax.tree.map(lambda a, e: jnp.zeros_like(a) + jnp.asarray(e, a.dtype), part, identity)

    def one(step, state):
        source = count - 1 - step if reverse else step
        return combine(
            state, jax.tree.map(lambda a: lax.dynamic_index_in_dim(a, source, 0, False), gathered)
        )

    return lax.fori_loop(0, ahead, one, state)


def product(left, right):
    return jnp.dot(left, right, precision=HIGH, preferred_element_type=jnp.float32)


def join_maps(earlier, later):
    return (product(earlier[0], later[0]), product(earlier[1], later[0]) + later[1])


def forward_step(state, blocks):
    rhs, coupling, inverse = blocks
    fresh = product(rhs - product(state, coupling), inverse)
    return (fresh, fresh)


def forward_compose_plain(acc, blocks):
    coupling, inverse = blocks
    return (-product(product(acc, coupling), inverse), None)


def backward_step(carry, blocks):
    state, coupling = blocks
    solved = state - carry
    return (product(solved, coupling), solved)


def backward_compose(acc, coupling):
    return (-product(acc, coupling), None)


def on_device(sketch, inv_diag, upper, lower):
    count = sketch.shape[0]
    columns = sketch.shape[1]
    width = sketch.shape[2]
    eye = jnp.eye(width, dtype=jnp.float32)
    blank = jnp.zeros((columns, width), jnp.float32)
    fwd_map, _ = lax.scan(forward_compose_plain, eye, (upper, inv_diag))
    fwd_end, zero_states = lax.scan(forward_step, blank, (sketch, upper, inv_diag))
    incoming = carried_in((fwd_map, fwd_end), "chain", join_maps, (eye, blank), False)[1]
    _, states = lax.scan(forward_step, incoming, (sketch, upper, inv_diag))
    back_map, _ = lax.scan(backward_compose, eye, lower, reverse=True)
    back_end, _ = lax.scan(backward_step, blank, (states, lower), reverse=True)
    from_above = carried_in((back_map, back_end), "chain", join_maps, (eye, blank), True)[1]
    _, solved = lax.scan(backward_step, from_above, (states, lower), reverse=True)
    local_gram = jnp.einsum("skb,slb->kl", solved, solved, precision=HIGH)
    total_gram = lax.psum(local_gram, "chain")
    gram = total_gram / (count * lax.axis_size("chain") * width)
    chol = jnp.linalg.cholesky(gram)
    identity = jnp.eye(columns, dtype=jnp.float32)
    inverse = lax.linalg.triangular_solve(chol, identity, left_side=True, lower=True)
    basis = jnp.einsum("kl,slb->skb", inverse, solved, precision=HIGH)
    return (basis, jnp.transpose(chol))


def solution(mesh):
    placed = (
        P("chain", None, None),
        P("chain", None, None),
        P("chain", None, None),
        P("chain", None, None),
    )
    return jax.shard_map(
        on_device,
        mesh=mesh,
        in_specs=placed,
        out_specs=(P("chain", None, None), P()),
        check_vma=False,
    )
```

profile of v0, /device:TPU:1, one launch (start us, length us, event | category | flops | bytes accessed | tf_op | source)
XLA Modules:
  0.0 677.5 jit_solution(16970784390179098600)
XLA Ops:
  7.2 4.9 while.104
  12.9 6.3 while.103
  12.9 1.5 fusion.96
  14.5 1.6 convolution_negate_fusion.3
  16.0 1.5 fusion.96
  17.6 1.6 convolution_negate_fusion.3
  20.1 3.2 while.102
  20.1 1.6 fusion.91
  21.7 1.6 fusion.91
  24.1 62.6 %all-gather.13.cloned.1.call-done = f32[8192,256]{1,0:T(8,128)} async-done(((f32[64,256]{1,0:T(8,128)}), f32[8192,256]{1,0:T(8,128)}) %all-gather.13.cloned.1.call-update) | async-done | bytes 8388624 | tf_op jit(solution)/shard_map/all_gather | solution.py:13
  86.7 107.3 %all-gather.11.cloned.1.call-done = f32[32768,256]{1,0:T(8,128)} async-done(((f32[256,256]{1,0:T(8,128)}), f32[32768,256]{1,0:T(8,128)}) %all-gather.11.cloned.1.call-update) | async-done | bytes 33554448 | tf_op jit(solution)/shard_map/all_gather | solution.py:13
  194.0 1.2 while.105
  195.3 4.9 while.106
  200.2 2.5 while.107
  203.4 118.0 %all-gather.9.cloned.1.call-done = f32[32768,256]{0,1:T(8,128)} async-done(((f32[256,256]{0,1:T(8,128)}), f32[32768,256]{0,1:T(8,128)}) %all-gather.9.cloned.1.call-update) | async-done | bytes 33554448 | tf_op jit(solution)/shard_map/all_gather | solution.py:13
  321.3 33.4 %copy.7 = f32[32768,256]{1,0:T(8,128)} copy(f32[32768,256]{0,1:T(8,128)} %all-gather.9.cloned.1.call-done) | data formatting | bytes 67108864 | tf_op jit(solution)/shard_map/all_gather | solution.py:13
  354.8 78.0 %all-gather.15.cloned.1.call-done = f32[8192,256]{1,0:T(8,128)} async-done(((f32[64,256]{1,0:T(8,128)}), f32[8192,256]{1,0:T(8,128)}) %all-gather.15.cloned.1.call-update) | async-done | bytes 8388624 | tf_op jit(solution)/shard_map/all_gather | solution.py:13
  432.8 160.3 %while.108 = (s32[]{:T(128)}, f32[64,256]{1,0:T(8,128)S(1)}, s32[]{:T(128)}, f32[128,256,256]{2,1,0:T(8,128)}, f32[128,64,256]{2,1,0:T(8,128)}, /*index=5*/s32[]{:T(128)}, s32[]{:T(128)}, s32[]{:T(128)}, s32[]{:T(128)}) while((s32[]{:T(128)}, f32[64,256]{1,0:T(8,128)S(1)}, s32[]{:T(128)}, f32[128,256,256]{2,1,0:T(8,128)}, ...), condition=%wide.region_13.14_spmd, body=%wide.region_12.13_spmd.sunk | while | flops 50348036 | bytes 590987 | solution.py:22
  451.9 1.2 fusion.114
  472.2 1.2 fusion.114
  492.6 1.2 fusion.114
  594.0 63.0 %psum.7 = f32[64,64]{0,1:T(8,128)S(1)} all-reduce(f32[64,64]{0,1:T(8,128)S(1)} %convolution_bitcast_fusion.6), channel_id=1, replica_groups=mesh['chain'=128] {'chain'}, use_global_device_ids=true, to_apply=%region_16.17 | all-reduce | flops 4096 | bytes 32768 | tf_op jit(solution)/shard_map/psum | solution.py:69
  657.1 5.8 cholesky.17
  664.2 4.9 custom-call.6
  (309 shorter events, 173.2 us)
Async XLA Ops:
  7.2 79.6 %all-gather.13.cloned.1.call-start = ((), (), s32[]{:S(2)}) async-start(), calls=%async_computation.2 | async-start | bytes 8454144 | tf_op jit(solution)/shard_map/all_gather | solution.py:13
  12.1 0.6 copy-start.3
  12.8 181.2 %all-gather.11.cloned.1.call-start = ((), (), s32[]{:S(2)}) async-start(), calls=%async_computation.1 | async-start | bytes 33816576 | tf_op jit(solution)/shard_map/all_gather | solution.py:13
  19.2 0.7 copy-start.2
  19.9 301.4 %all-gather.9.cloned.1.call-start = ((), (), s32[]{:S(2)}) async-start(), calls=%async_computation | async-start | bytes 33816576 | tf_op jit(solution)/shard_map/all_gather | solution.py:13
  23.3 0.7 copy-start.1
  24.0 408.7 %all-gather.15.cloned.1.call-start = ((), (), s32[]{:S(2)}) async-start(), calls=%async_computation.3 | async-start | bytes 8454144 | tf_op jit(solution)/shard_map/all_gather | solution.py:13
  202.7 0.6 copy-start.4
  203.4 389.7 %copy-start = (f32[2,256,256]{2,1,0:T(8,128)S(1)}, f32[2,256,256]{2,1,0:T(8,128)}, u32[]{:S(2)}) copy-start(f32[2,256,256]{2,1,0:T(8,128)} %get-tuple-element.950) | copy-start | bytes 1572868
Sparse Core Ops, SparseCore 0:
  12.9 73.7 all-gather.12
  89.7 104.2 all-gather.10
  196.9 124.4 all-gather.8
  324.7 107.9 all-gather.14
where the time goes:
time: 681 us; the launch traced here: 678 us
  waiting for transfers between devices  366 us (54%)
  matrix products  179 us (26%)
  blocking collectives  63 us (9%)
  local copies, waits for them, and re-layouts  37.9 us (6%)
  between operations  14 us (2%)
  other arithmetic  12.1 us (2%)
    all_gather x4, waiting for transfers between devices, carried_in(): gathered = jax.tree.map(lambda a: lax.all_gather(a, axis), part)  366 us
    dot_general x145, matrix products, product(): jnp.dot(left, right, precision=HIGH, preferred_element_type=jnp.float32)  178 us
    psum x1, blocking collectives, on_device(): total_gram = lax.psum(local_gram, 'chain')  63 us
    all_gather x1, local copies, waits for them, and re-layouts, carried_in(): gathered = jax.tree.map(lambda a: lax.all_gather(a, axis), part)  33.4 us
  transfers between devices with their start and end apart: 4, of which 4 were waited for; matrix products, arithmetic and copies ran while one was open for 8% of the time, Pallas kernels for 0%

commit v1 on v0

--- a/solution.py
+++ b/solution.py
@@ -66,7 +66,8 @@
     from_above = carried_in((back_map, back_end), "chain", join_maps, (eye, blank), True)[1]
     _, solved = lax.scan(backward_step, from_above, (states, lower), reverse=True)
     local_gram = jnp.einsum("skb,slb->kl", solved, solved, precision=HIGH)
-    total_gram = lax.psum(local_gram, "chain")
+    parts = lax.all_gather(local_gram, "chain", axis=0, tiled=False)
+    total_gram = parts.sum(axis=0)
     gram = total_gram / (count * lax.axis_size("chain") * width)
     chol = jnp.linalg.cholesky(gram)
     identity = jnp.eye(columns, dtype=jnp.float32)

time: 681 us -> 683 us (level)
  blocking collectives: 63 us -> 0 us
  waiting for transfers between devices: 366 us -> 428 us
    psum x1 -> x0, blocking collectives: 63 us -> none  [on_device(): total_gram = lax.psum(local_gram, 'chain')]
    all_gather x0 -> x1, waiting for transfers between devices: none -> 61.7 us  [on_device(): parts = lax.all_gather(local_gram, 'chain', axis=0, tiled=False)]
  transfers between devices with their start and end apart: 4 -> 5, of which waited for: 4 -> 5; matrix products, arithmetic and copies ran while one was open for 8% -> 8% of each run, Pallas kernels for 0% -> 0%
where the time goes in v1:
time: 683 us; the launch traced here: 679 us
  waiting for transfers between devices  428 us (63%)
  matrix products  180 us (26%)
  local copies, waits for them, and re-layouts  38 us (6%)
  other arithmetic  14.7 us (2%)
  between operations  14 us (2%)
    all_gather x4, waiting for transfers between devices, carried_in(): gathered = jax.tree.map(lambda a: lax.all_gather(a, axis), part)  366 us
    dot_general x145, matrix products, product(): jnp.dot(left, right, precision=HIGH, preferred_element_type=jnp.float32)  178 us
    all_gather x1, waiting for transfers between devices, on_device(): parts = lax.all_gather(local_gram, 'chain', axis=0, tiled=False)  61.7 us
    all_gather x1, local copies, waits for them, and re-layouts, carried_in(): gathered = jax.tree.map(lambda a: lax.all_gather(a, axis), part)  33.4 us
  transfers between devices with their start and end apart: 5, of which 5 were waited for; matrix products, arithmetic and copies ran while one was open for 8% of the time, Pallas kernels for 0%

profile of v1, /device:TPU:1, one launch (start us, length us, event | category | flops | bytes accessed | tf_op | source)
XLA Modules:
  0.0 679.4 jit_solution(2427318953406942483)
XLA Ops:
  7.2 4.9 while.104
  12.9 6.3 while.103
  12.9 1.5 fusion.96
  14.5 1.6 convolution_negate_fusion.3
  16.0 1.5 fusion.96
  17.6 1.6 convolution_negate_fusion.3
  20.1 3.2 while.102
  20.1 1.6 fusion.91
  21.7 1.6 fusion.91
  24.1 62.6 %all-gather.15.cloned.1.call-done = f32[8192,256]{1,0:T(8,128)} async-done(((f32[64,256]{1,0:T(8,128)}), f32[8192,256]{1,0:T(8,128)}) %all-gather.15.cloned.1.call-update) | async-done | bytes 8388624 | tf_op jit(solution)/shard_map/all_gather | solution.py:13
  86.7 107.3 %all-gather.13.cloned.1.call-done = f32[32768,256]{1,0:T(8,128)} async-done(((f32[256,256]{1,0:T(8,128)}), f32[32768,256]{1,0:T(8,128)}) %all-gather.13.cloned.1.call-update) | async-done | bytes 33554448 | tf_op jit(solution)/shard_map/all_gather | solution.py:13
  194.0 1.2 while.105
  195.3 4.9 while.106
  200.2 2.5 while.107
  203.4 117.9 %all-gather.11.cloned.1.call-done = f32[32768,256]{0,1:T(8,128)} async-done(((f32[256,256]{0,1:T(8,128)}), f32[32768,256]{0,1:T(8,128)}) %all-gather.11.cloned.1.call-update) | async-done | bytes 33554448 | tf_op jit(solution)/shard_map/all_gather | solution.py:13
  321.3 33.4 %copy.11 = f32[32768,256]{1,0:T(8,128)} copy(f32[32768,256]{0,1:T(8,128)} %all-gather.11.cloned.1.call-done) | data formatting | bytes 67108864 | tf_op jit(solution)/shard_map/all_gather | solution.py:13
  354.8 78.0 %all-gather.17.cloned.1.call-done = f32[8192,256]{1,0:T(8,128)} async-done(((f32[64,256]{1,0:T(8,128)}), f32[8192,256]{1,0:T(8,128)}) %all-gather.17.cloned.1.call-update) | async-done | bytes 8388624 | tf_op jit(solution)/shard_map/all_gather | solution.py:13
  432.8 160.3 %while.108 = (s32[]{:T(128)}, f32[64,256]{1,0:T(8,128)S(1)}, s32[]{:T(128)}, f32[128,256,256]{2,1,0:T(8,128)}, f32[128,64,256]{2,1,0:T(8,128)}, /*index=5*/s32[]{:T(128)}, s32[]{:T(128)}, s32[]{:T(128)}, s32[]{:T(128)}) while((s32[]{:T(128)}, f32[64,256]{1,0:T(8,128)S(1)}, s32[]{:T(128)}, f32[128,256,256]{2,1,0:T(8,128)}, ...), condition=%wide.region_13.14_spmd, body=%wide.region_12.13_spmd.sunk | while | flops 50348036 | bytes 590987 | solution.py:22
  443.0 1.2 fusion.114
  463.3 1.2 fusion.114
  594.6 61.7 %all-gather.19.cloned.1.call-done = f32[8192,64]{1,0:T(8,128)} async-done(((f32[64,64]{1,0:T(8,128)}), f32[8192,64]{1,0:T(8,128)}) %all-gather.19.cloned.1.call-update) | async-done | bytes 2097168 | tf_op jit(solution)/shard_map/all_gather | solution.py:69
  656.3 2.5 reduce_sum.11
  658.9 5.8 cholesky.17
  666.1 4.9 custom-call.6
  (311 shorter events, 175.1 us)
Async XLA Ops:
  7.2 79.6 %all-gather.15.cloned.1.call-start = ((), (), s32[]{:S(2)}) async-start(), calls=%async_computation.2 | async-start | bytes 8454144 | tf_op jit(solution)/shard_map/all_gather | solution.py:13
  12.1 0.6 copy-start.3
  12.8 181.2 %all-gather.13.cloned.1.call-start = ((), (), s32[]{:S(2)}) async-start(), calls=%async_computation.1 | async-start | bytes 33816576 | tf_op jit(solution)/shard_map/all_gather | solution.py:13
  19.2 0.7 copy-start.2
  19.9 301.4 %all-gather.11.cloned.1.call-start = ((), (), s32[]{:S(2)}) async-start(), calls=%async_computation | async-start | bytes 33816576 | tf_op jit(solution)/shard_map/all_gather | solution.py:13
  23.3 0.7 copy-start.1
  24.1 408.7 %all-gather.17.cloned.1.call-start = ((), (), s32[]{:S(2)}) async-start(), calls=%async_computation.3 | async-start | bytes 8454144 | tf_op jit(solution)/shard_map/all_gather | solution.py:13
  202.7 0.6 copy-start.4
  203.4 452.9 %all-gather.19.cloned.1.call-start = ((), (), s32[]{:S(2)}) async-start(), calls=%async_computation.4 | async-start | bytes 4227072 | tf_op jit(solution)/shard_map/all_gather | solution.py:69
  203.4 389.7 %copy-start = (f32[2,256,256]{2,1,0:T(8,128)S(1)}, f32[2,256,256]{2,1,0:T(8,128)}, u32[]{:S(2)}) copy-start(f32[2,256,256]{2,1,0:T(8,128)} %get-tuple-element.956) | copy-start | bytes 1572868
Sparse Core Ops, SparseCore 0:
  12.9 73.7 all-gather.14
  89.7 104.2 all-gather.12
  196.9 124.4 all-gather.10
  324.7 107.9 all-gather.16
  594.8 61.4 all-gather.18
